TPU v7x, 32 devices: a whole 2x2x4 slice. The times are simulated.
32 devices in a mesh: groups: 2 (over y), scen: 4 (over z), tile: 4 (over x, core).
Axes of the slice: x: 2, y: 2, z: 4, core: 2. Of those that a mesh axis runs over, the one named last changes fastest.
Arguments:
- linking: bfloat16 [64, 256, 1024], P(('groups', 'scen', 'tile')), parts along dimension 0, may hold values from -0.029907227 to 0.029907227
- scaling: float32 [64, 256], P(('groups', 'scen', 'tile')), parts along dimension 0, may hold values from 0.25 to 4
- residual: float32 [64, 256], P(('groups', 'scen', 'tile')), parts along dimension 0, may hold values from -6 to 6
- blocks: int32 [64, 8], P('groups'), parts along dimension 0, may hold values from 0 to 63, as said below
- step_dx: float32 [128, 128], P(('groups', 'scen')), parts along dimension 0, may hold values from -24 to 24
- first_diag: float32 [16384], P(('groups', 'scen')), parts along dimension 0, may hold values from 0.5 to 1.5
Outputs:
- schur: float32 [16384, 8192], P(('groups', 'scen'), 'tile'), parts along dimension 0
- back_step: float32 [64, 256], P(('groups', 'scen', 'tile')), parts along dimension 0
There are 2 independent parts, one for each index of `groups`. A program takes and returns all parts, laid end to end along the dimension named above; each array names one. Nothing has to cross between parts.
Inputs may be any that keep to these rules, and one draw needn't show every extreme that they name: Position k of every list names a block of column group g = k mod 4, a number from g * 16 to g * 16 + 15; within its group the block lies in one of 1 runs of 16 consecutive blocks, and its number modulo 16 lies from (k // 4) * (8) to that plus 16 // 2 - 1, so the blocks of a list are distinct. Among the 8 scenarios of one scen shard (aligned runs of 8 scenarios), at each position at most 8 name a block of the same run; in every shard and at every position of a group one run, the same for the whole group and all shards, is named exactly 8 times, and the other runs share the rest as evenly as possible.
All inputs are finite; a program needn't handle non-finite values.
Results may differ from a plain program's by a relative error of at most 0.0012.
The roundings to bfloat16 on the way count: a program that leaves them out, or rounds other values in their place, can miss the bound.
Values may be sent and summed in bfloat16 or wider, within the bound.
A program may use at most 64 MiB of HBM per device.

v0:
```python
import jax
import jax.numpy as jnp
from jax import lax
from jax.sharding import PartitionSpec as P

BW = 128
LIST = 8
NBLK = 64


def on_device(linking, scaling, residual, blocks, step_dx, first_diag):
    tiles_ax = lax.axis_size("tile")
    scen_ax = lax.axis_size("scen")
    here_scen = lax.axis_index("scen")
    here_tile = lax.axis_index("tile")
    held_scen = linking.shape[0]
    shard_size = tiles_ax * held_scen
    width_rows = step_dx.shape[0]
    width_cols = NBLK // tiles_ax
    per_group = LIST // tiles_ax
    owners_per = scen_ax // tiles_ax
    cap_owner = min(shard_size, (3 * shard_size + 2 * owners_per - 1) // (2 * owners_per))
    slot_count = per_group * per_group * cap_owner
    target_count = width_rows * width_cols
    own_blocks = lax.dynamic_slice_in_dim(
        blocks, (here_scen * tiles_ax + here_tile) * held_scen, held_scen, 0
    )
    low_step = step_dx.astype(jnp.bfloat16)
    full_step = lax.all_gather(low_step, "scen", axis=0, tiled=True)
    picked = full_step[own_blocks].reshape(held_scen, LIST * BW)
    applied = jnp.einsum("src,sc->sr", linking, picked, preferred_element_type=jnp.float32)
    back_step = scaling * (residual - applied)
    scaled = (jnp.sqrt(scaling)[:, :, None] * linking).astype(jnp.bfloat16)
    gram_full = jnp.einsum("sra,src->sac", scaled, scaled, preferred_element_type=jnp.float32)
    gram_tiles = (
        gram_full.reshape(held_scen, LIST, BW, LIST, BW)
        .transpose(0, 1, 3, 2, 4)
        .astype(jnp.bfloat16)
    )
    outgoing = gram_tiles.reshape(held_scen, LIST, per_group, tiles_ax, BW, BW).transpose(
        3, 0, 2, 1, 4, 5
    )
    incoming = lax.all_to_all(outgoing, "tile", split_axis=0, concat_axis=0, tiled=True)
    flat_tiles = incoming.reshape(shard_size * per_group * LIST, BW, BW)
    shard_blocks = blocks.reshape(scen_ax, shard_size, LIST)

    def route_tiles(block_lists):
        col_blocks = jnp.take(block_lists, jnp.arange(per_group) * tiles_ax + here_tile, axis=1)
        row_block = jnp.broadcast_to(
            block_lists[:, None, :], (shard_size, per_group, LIST)
        ).reshape(-1)
        col_block = jnp.broadcast_to(col_blocks[:, :, None], (shard_size, per_group, LIST)).reshape(
            -1
        )
        owner_idx = row_block // width_rows
        hit_table = (owner_idx[:, None] == jnp.arange(scen_ax)[None, :]).astype(jnp.int32)
        before = jnp.cumsum(hit_table, axis=0) - hit_table
        slot_rank = jnp.sum(before * hit_table, axis=1)
        target = row_block % width_rows * width_cols + col_block % width_cols
        return (owner_idx, slot_rank, target)

    own_lists = lax.dynamic_index_in_dim(shard_blocks, here_scen, 0, keepdims=False)
    send_owner, send_rank, unused = route_tiles(own_lists)
    outbox = (
        jnp.zeros((scen_ax, slot_count, BW, BW), jnp.bfloat16)
        .at[send_owner, send_rank]
        .set(flat_tiles)
    )
    received = lax.all_to_all(outbox, "scen", split_axis=0, concat_axis=0, tiled=True)
    all_owner, all_rank, all_target = jax.vmap(route_tiles)(shard_blocks)
    is_mine = all_owner == here_scen
    slot_id = jnp.arange(scen_ax)[:, None] * slot_count + all_rank
    pick_target = (
        (all_target[:, :, None] == jnp.arange(target_count)[None, None, :]) & is_mine[:, :, None]
    ).astype(jnp.float32)
    pick_slot = (slot_id[:, :, None] == jnp.arange(scen_ax * slot_count)[None, None, :]).astype(
        jnp.float32
    )
    select = jnp.einsum("pnt,pnz->tz", pick_target, pick_slot).astype(jnp.bfloat16)
    summed = jnp.dot(
        select, received.reshape(scen_ax * slot_count, BW * BW), preferred_element_type=jnp.float32
    )
    schur_block = (
        summed.reshape(width_rows, width_cols, BW, BW)
        .transpose(0, 2, 1, 3)
        .reshape(width_rows * BW, width_cols * BW)
    )
    rows_global = here_scen * (width_rows * BW) + jnp.arange(width_rows * BW)
    cols_global = here_tile * (width_cols * BW) + jnp.arange(width_cols * BW)
    schur_block = schur_block + jnp.where(
        rows_global[:, None] == cols_global[None, :], first_diag[:, None], 0.0
    )
    return (schur_block, back_step)


def solution(mesh):
    in_specs = (
        P(("groups", "scen", "tile"), None, None),
        P(("groups", "scen", "tile"), None),
        P(("groups", "scen", "tile"), None),
        P("groups", None),
        P(("groups", "scen"), None),
        P(("groups", "scen")),
    )
    out_specs = (P(("groups", "scen"), "tile"), P(("groups", "scen", "tile"), None))
    return jax.shard_map(
        on_device, mesh=mesh, in_specs=in_specs, out_specs=out_specs, check_vma=False
    )
```

profile of v0, /device:TPU:0, one launch (start us, length us, event | category | flops | bytes accessed | tf_op | source)
XLA Modules:
  0.0 235.6 jit_solution(6924571524478192047)
XLA Ops:
  0.6 0.8 compare_select_fusion
  1.4 0.1 copy.33
  1.5 0.1 reshape.300
  1.6 0.7 convert_element_type.37
  2.3 14.8 %all_gather.3 = bf16[64,128]{1,0:T(8,128)(2,1)S(1)} all-gather(bf16[16,128]{1,0:T(8,128)(2,1)S(1)} %convert_element_type.37), channel_id=1, replica_groups=mesh['groups'=2,'scen'=4,'tile'=4] {'scen'}, dimensions={0}, use_global_device_ids=true | all-gather | bytes 20480 | tf_op jit(solution)/shard_map/all_gather | solution.py:29
  17.1 0.6 gather_fusion.1
  17.7 1.6 fusion.18
  19.3 1.3 fusion.12
  20.5 3.0 %convolution_convert_fusion = bf16[2,1024,1024]{2,1,0:T(8,128)(2,1)S(1)} fusion(bf16[2,256,1024]{2,1,0:T(8,128)(2,1)} %param.6, f32[2,256]{1,0:T(2,128)S(1)} %get-tuple-element.5), kind=kOutput, calls=%fused_computation.5 | convolution fusion | flops 1077411840 | bytes 5244928 | tf_op jit(solution)/shard_map/sra,src->sac/dot_general | solution.py:34
  23.6 1.1 copy.38
  24.7 1.2 copy.29
  25.9 2.3 copy.30
  28.2 0.0 copy-start
  28.2 5.0 %all-to-all-start = ((bf16[4,2,2,8,128,128]{5,4,2,3,1,0:T(8,128)(2,1)}), bf16[4,2,2,8,128,128]{5,4,2,3,1,0:T(8,128)(2,1)}, u32[]{:S(2)}, u32[]{:S(2)}) async-start(bf16[4,2,2,8,128,128]{5,4,2,3,1,0:T(8,128)(2,1)} %copy.30), calls=%async_computation | async-start | bytes 8388608 | tf_op jit(solution)/shard_map/all_to_all | solution.py:43
  33.2 0.0 copy-done
  33.3 0.1 broadcast_in_dim.32
  33.3 0.1 copy.27
  33.4 0.1 reshape.284
  33.5 0.1 reshape.283
  33.6 0.1 fusion.8
  33.7 0.2 reduce_window_sum.23
  33.9 0.2 select_reduce_fusion.1
  34.1 47.4 %all-to-all-done = bf16[4,2,2,8,128,128]{5,4,2,3,1,0:T(8,128)(2,1)} async-done(((bf16[4,2,2,8,128,128]{5,4,2,3,1,0:T(8,128)(2,1)}), bf16[4,2,2,8,128,128]{5,4,2,3,1,0:T(8,128)(2,1)}, u32[]{:S(2)}, u32[]{:S(2)}) %all-to-all-start) | async-done | bytes 4194336 | tf_op jit(solution)/shard_map/all_to_all | solution.py:43
  81.5 4.7 %copy.31 = bf16[4,2,2,8,128,128]{5,4,3,2,1,0:T(8,128)(2,1)} copy(bf16[4,2,2,8,128,128]{5,4,2,3,1,0:T(8,128)(2,1)} %all-to-all-done) | data formatting | bytes 8388608 | tf_op jit(solution)/shard_map/all_to_all | solution.py:43
  86.2 3.1 %broadcast_in_dim.37 = bf16[4,32,128,128]{3,2,1,0:T(8,128)(2,1)} broadcast(bf16[]{:T(256)} %constant.92.clone.1), dimensions={} | broadcast | bytes 4194306 | tf_op jit(solution)/shard_map/broadcast_in_dim | solution.py:65
  89.3 20.7 %scatter_fusion = bf16[4,32,128,128]{3,2,1,0:T(8,128)(2,1)} fusion(bf16[4,32,128,128]{3,2,1,0:T(8,128)(2,1)} %broadcast_in_dim.37, s32[128]{0:T(128)S(1)} %fusion.16, bf16[128,128,128]{2,1,0:T(8,128)(2,1)} %bitcast.58), kind=kCustom, calls=%fused_computation.2 | custom fusion | bytes 12583936 | tf_op jit(solution)/shard_map/scatter | solution.py:67
  110.0 5.0 %all-to-all-start.1 = ((bf16[4,32,128,128]{3,2,1,0:T(8,128)(2,1)}), bf16[4,32,128,128]{3,2,1,0:T(8,128)(2,1)}, u32[]{:S(2)}, u32[]{:S(2)}) async-start(bf16[4,32,128,128]{3,2,1,0:T(8,128)(2,1)} %scatter_fusion), calls=%async_computation.1 | async-start | bytes 8388608 | tf_op jit(solution)/shard_map/all_to_all | solution.py:69
  115.0 0.1 copy.25
  115.1 0.6 gather_fusion
  115.7 0.1 select_bitcast_fusion
  115.8 0.1 copy.26
  115.9 0.1 broadcast_in_dim.36
  116.0 0.1 reshape.282
  116.1 0.1 reshape.281
  116.2 0.1 fusion.4
  116.4 0.3 reduce_window_sum.22
  116.7 0.2 select_reduce_fusion
  116.9 0.1 fusion.10
  117.0 0.3 fusion
  117.3 90.8 %all-to-all-done.1 = bf16[4,32,128,128]{3,2,1,0:T(8,128)(2,1)} async-done(((bf16[4,32,128,128]{3,2,1,0:T(8,128)(2,1)}), bf16[4,32,128,128]{3,2,1,0:T(8,128)(2,1)}, u32[]{:S(2)}, u32[]{:S(2)}) %all-to-all-start.1) | async-done | bytes 4194336 | tf_op jit(solution)/shard_map/all_to_all | solution.py:69
  208.1 7.7 %copy.44 = bf16[16,8,128,128]{3,1,2,0:T(8,128)(2,1)} copy(bf16[16,8,128,128]{3,2,1,0:T(8,128)(2,1)} %bitcast.29) | data formatting | bytes 8388608
  215.9 6.4 %copy.32 = bf16[16384,128]{1,0:T(8,128)(2,1)} copy(bf16[16384,128]{0,1:T(8,128)(2,1)} %bitcast.62) | data formatting | bytes 8388608 | tf_op jit(solution)/shard_map/dot_general | solution.py:80
  222.3 0.0 copy-start.1
  222.3 4.5 %fusion.17 = f32[16,16,128,128]{3,1,2,0:T(8,128)S(1)} fusion(bf16[16,16,128,1]{2,1,3,0:T(8,128)(2,1)S(1)} %bitcast.64, bf16[128,128,128,1]{2,1,0,3:T(8,128)(2,1)} %bitcast.63), kind=kOutput, calls=%fused_computation.67 | convolution fusion | flops 1073741824 | bytes 21037056 | tf_op jit(solution)/shard_map/dot_general | solution.py:80
  226.8 0.0 copy-done.1
  226.8 8.8 %bitcast_add_fusion = f32[2048,2048]{1,0:T(8,128)} fusion(f32[256,8,16,128]{3,2,1,0:T(8,128)S(1)} %bitcast.57, f32[2048]{0:T(1024)S(1)} %copy-done.1, s32[2048]{0:T(1024)S(1)} %get-tuple-element.8, s32[2048]{0:T(1024)S(1)} %get-tuple-element.9), kind=kLoop, calls=%fused_computation.3 | loop fusion | flops 12582912 | bytes 33579008 | tf_op jit(solution)/shard_map/add | solution.py:90
  (13 shorter events, 0.1 us)
Async XLA Ops:
  28.2 5.0 %copy-start = (s32[32,8]{0,1:T(8,128)S(1)}, s32[32,8]{0,1:T(8,128)}, u32[]{:S(2)}) copy-start(s32[32,8]{0,1:T(8,128)} %param.9) | copy-start | bytes 3076
  28.2 53.2 %all-to-all-start = ((bf16[4,2,2,8,128,128]{5,4,2,3,1,0:T(8,128)(2,1)}), bf16[4,2,2,8,128,128]{5,4,2,3,1,0:T(8,128)(2,1)}, u32[]{:S(2)}, u32[]{:S(2)}) async-start(bf16[4,2,2,8,128,128]{5,4,2,3,1,0:T(8,128)(2,1)} %copy.30), calls=%async_computation | async-start | bytes 8388608 | tf_op jit(solution)/shard_map/all_to_all | solution.py:43
  110.0 98.1 %all-to-all-start.1 = ((bf16[4,32,128,128]{3,2,1,0:T(8,128)(2,1)}), bf16[4,32,128,128]{3,2,1,0:T(8,128)(2,1)}, u32[]{:S(2)}, u32[]{:S(2)}) async-start(bf16[4,32,128,128]{3,2,1,0:T(8,128)(2,1)} %scatter_fusion), calls=%async_computation.1 | async-start | bytes 8388608 | tf_op jit(solution)/shard_map/all_to_all | solution.py:69
  222.3 4.6 %copy-start.1 = (f32[2048]{0:T(1024)S(1)}, f32[2048]{0:T(1024)}, u32[]{:S(2)}) copy-start(f32[2048]{0:T(1024)} %param.11) | copy-start | bytes 24580
where the time goes:
time: 236 us
  waiting for transfers between devices  138 us (58%)
  local copies, waits for them, and re-layouts  49.5 us (21%)
  blocking collectives  14.8 us (6%)
  other arithmetic  12.8 us (5%)
  starting transfers between devices  10 us (4%)
  matrix products  9.49 us (4%)
    all_to_all x1, waiting for transfers between devices, on_device(): lax.all_to_all(outbox, 'scen', split_axis=0, concat_axis=0, tiled=True)  90.8 us
    all_to_all x1, waiting for transfers between devices, on_device(): lax.all_to_all(outgoing, 'tile', split_axis=0, concat_axis=0, tiled=True)  47.4 us
    scatter x1, local copies, waits for them, and re-layouts, on_device(): outbox = jnp.zeros((scen_ax, slot_count, BW, BW), jnp.bfloat16).at[send_o...  20.7 us
    all_gather x1, blocking collectives, on_device(): full_step = lax.all_gather(low_step, 'scen', axis=0, tiled=True)  14.8 us
    unnamed x6, local copies, waits for them, and re-layouts  8.84 us
    add x1, other arithmetic, on_device(): schur_block + jnp.where(rows_global[:, None] == cols_global[None, :], fir...  8.76 us
    dot_general x1, local copies, waits for them, and re-layouts, on_device(): jnp.dot(select, received.reshape(scen_ax * slot_count, BW * BW), preferre...  6.39 us
    all_to_all x1, starting transfers between devices, on_device(): lax.all_to_all(outbox, 'scen', split_axis=0, concat_axis=0, tiled=True)  5.04 us
  transfers between devices with their start and end apart: 2, of which 2 were waited for; matrix products, arithmetic and copies ran while one was open for 1% of the time, Pallas kernels for 0%

commit v1 on v0

--- a/solution.py
+++ b/solution.py
@@ -1,6 +1,10 @@
+import functools
+
 import jax
 import jax.numpy as jnp
 from jax import lax
+from jax.experimental import pallas as pl
+from jax.experimental.pallas import tpu as pltpu
 from jax.sharding import PartitionSpec as P
 
 BW = 128
@@ -93,6 +97,314 @@
     return (schur_block, back_step)
 
 
+MESH = pl.DeviceIdType.MESH
+
+
+def exchange_kernel(
+    n, held, scaled_ref, step_ref, got_ref, steps_ref,
+    gathered, parts, step_box,
+    load_sem, own_sem, pass_sem, chain_sem, part_sem, got_sem, keep_sem, step_sem, step_got_sem,
+):
+    z = lax.axis_index("scen")
+    t = lax.axis_index("tile")
+
+    def load(j):
+        return pltpu.make_async_copy(scaled_ref.at[j], gathered.at[z, j], load_sem.at[j])
+
+    def hop(source, j, sem, to):
+        return pltpu.make_async_remote_copy(
+            src_ref=gathered.at[source, j],
+            dst_ref=gathered.at[source, j],
+            send_sem=sem,
+            recv_sem=chain_sem.at[source, j],
+            device_id={"scen": to},
+            device_id_type=MESH,
+        )
+
+    def part_send(q, d):
+        to = lax.rem(t + d, n)
+        return pltpu.make_async_remote_copy(
+            src_ref=parts.at[q, to],
+            dst_ref=got_ref.at[t, q],
+            send_sem=part_sem.at[q, d - 1],
+            recv_sem=got_sem.at[t, q],
+            device_id={"tile": to},
+            device_id_type=MESH,
+        )
+
+    def part_arrival(source, q):
+        return pltpu.make_async_remote_copy(
+            src_ref=parts.at[q, source],
+            dst_ref=got_ref.at[source, q],
+            send_sem=part_sem.at[q, 0],
+            recv_sem=got_sem.at[source, q],
+            device_id={"tile": source},
+            device_id_type=MESH,
+        )
+
+    def part_keep(q):
+        return pltpu.make_async_copy(parts.at[q, t], got_ref.at[t, q], keep_sem.at[q])
+
+    def step_send(d):
+        to = lax.rem(z + d, n)
+        return pltpu.make_async_remote_copy(
+            src_ref=step_box.at[z],
+            dst_ref=step_box.at[z],
+            send_sem=step_sem.at[d - 1],
+            recv_sem=step_got_sem.at[z],
+            device_id={"scen": to},
+            device_id_type=MESH,
+        )
+
+    def step_arrival(d):
+        source = lax.rem(z + d, n)
+        return pltpu.make_async_remote_copy(
+            src_ref=step_box.at[source],
+            dst_ref=step_box.at[source],
+            send_sem=step_sem.at[d - 1],
+            recv_sem=step_got_sem.at[source],
+            device_id={"scen": source},
+            device_id_type=MESH,
+        )
+
+    def gram(source, j):
+        q = source * held + j
+        block = gathered.at[source, j]
+        left = jnp.concatenate(
+            [
+                block[:, pl.ds(pl.multiple_of((z + a * n) * BW, BW), BW)]
+                for a in range(2)
+            ],
+            axis=1,
+        )
+        turned = left.T
+        for to in range(n):
+            right = jnp.concatenate(
+                [block[:, (to + b * n) * BW : (to + b * n + 1) * BW] for b in range(2)], axis=1
+            )
+            parts[q, to] = jnp.dot(turned, right, preferred_element_type=jnp.float32).astype(
+                jnp.bfloat16
+            )
+        for d in range(1, n):
+            part_send(q, d).start()
+        part_keep(q).start()
+
+    for j in range(held):
+        load(j).start()
+    barrier = pltpu.get_barrier_semaphore()
+    for d in range(1, n):
+        pl.semaphore_signal(
+            barrier, inc=1, device_id={"scen": lax.rem(z + d, n)}, device_id_type=MESH
+        )
+        pl.semaphore_signal(
+            barrier, inc=1, device_id={"tile": lax.rem(t + d, n)}, device_id_type=MESH
+        )
+    step_box[z] = step_ref[...].astype(jnp.bfloat16)
+    pl.semaphore_wait(barrier, 2 * (n - 1))
+
+    for j in range(held):
+        load(j).wait()
+
+        @pl.when(z < n - 1)
+        def _():
+            hop(z, j, own_sem.at[0, j], z + 1).start()
+
+        @pl.when(z > 0)
+        def _():
+            hop(z, j, own_sem.at[1, j], z - 1).start()
+
+    for d in range(1, n):
+        step_send(d).start()
+
+    @pl.loop(0, held)
+    def _(j):
+        gram(z, j)
+
+    @pl.loop(0, 2 * held * (n - 1))
+    def _(i):
+        d = 1 + i // (2 * held)
+        j = (i // 2) % held
+        way = 1 - 2 * (i % 2)
+        source = z - way * d
+        onward = z + way
+
+        @pl.when((source >= 0) & (source < n))
+        def _():
+            hop(source, j, pass_sem.at[source, j], z).wait_recv()
+
+            @pl.when((onward >= 0) & (onward < n))
+            def _():
+                hop(source, j, pass_sem.at[source, j], onward).start()
+
+            gram(source, j)
+
+    for d in range(1, n):
+        step_send(d).wait_send()
+        step_arrival(d).wait_recv()
+    steps_ref[...] = step_box[...].reshape(steps_ref.shape)
+
+    for j in range(held):
+
+        @pl.when(z < n - 1)
+        def _():
+            hop(z, j, own_sem.at[0, j], z + 1).wait_send()
+
+        @pl.when(z > 0)
+        def _():
+            hop(z, j, own_sem.at[1, j], z - 1).wait_send()
+
+    @pl.loop(0, 2 * held * (n - 1))
+    def _(i):
+        d = 1 + i // (2 * held)
+        j = (i // 2) % held
+        way = 1 - 2 * (i % 2)
+        source = z - way * d
+        onward = z + way
+
+        @pl.when((source >= 0) & (source < n) & (onward >= 0) & (onward < n))
+        def _():
+            hop(source, j, pass_sem.at[source, j], onward).wait_send()
+
+    @pl.loop(0, n * held)
+    def _(q):
+        part_keep(q).wait()
+        for d in range(1, n):
+            part_send(q, d).wait_send()
+            part_arrival(lax.rem(t + d, n), q).wait_recv()
+
+
+def exchange(n, scaled, step_dx):
+    held, rows, width = scaled.shape
+    return pl.pallas_call(
+        functools.partial(exchange_kernel, n, held),
+        out_shape=(
+            jax.ShapeDtypeStruct((n, n * held, 2 * BW, 2 * BW), jnp.bfloat16),
+            jax.ShapeDtypeStruct((n * step_dx.shape[0], BW), jnp.bfloat16),
+        ),
+        in_specs=[pl.BlockSpec(memory_space=pl.ANY), pl.BlockSpec(memory_space=pltpu.VMEM)],
+        out_specs=(pl.BlockSpec(memory_space=pl.ANY), pl.BlockSpec(memory_space=pltpu.VMEM)),
+        scratch_shapes=[
+            pltpu.VMEM((n, held, rows, width), jnp.bfloat16),
+            pltpu.VMEM((n * held, n, 2 * BW, 2 * BW), jnp.bfloat16),
+            pltpu.VMEM((n,) + step_dx.shape, jnp.bfloat16),
+            pltpu.SemaphoreType.DMA((held,)),
+            pltpu.SemaphoreType.DMA((2, held)),
+            pltpu.SemaphoreType.DMA((n, held)),
+            pltpu.SemaphoreType.DMA((n, held)),
+            pltpu.SemaphoreType.DMA((n * held, n - 1)),
+            pltpu.SemaphoreType.DMA((n, n * held)),
+            pltpu.SemaphoreType.DMA((n * held,)),
+            pltpu.SemaphoreType.DMA((n - 1,)),
+            pltpu.SemaphoreType.DMA((n,)),
+        ],
+        compiler_params=pltpu.CompilerParams(
+            collective_id=0, has_side_effects=True, vmem_limit_bytes=40 * 2**20
+        ),
+        name="exchange",
+    )(scaled, step_dx)
+
+
+def assemble_kernel(
+    n, held, cap, blocks_ref, got_ref, diag_ref, steps_ref, linking_ref, scaling_ref, residual_ref,
+    schur_ref, back_ref, box, total, wide, in_sem, out_sem,
+):
+    z = lax.axis_index("scen")
+    t = lax.axis_index("tile")
+    half = cap // 2
+
+    def load(a):
+        return pltpu.make_async_copy(
+            got_ref.at[:, :, pl.ds(a * BW, BW)], box.at[a], in_sem.at[a]
+        )
+
+    def store(a):
+        rows = pl.ds(a * half * BW, half * BW)
+        return pltpu.make_async_copy(total.at[rows], schur_ref.at[rows], out_sem.at[a])
+
+    load(0).start()
+    load(1).start()
+    on_diagonal = lax.broadcasted_iota(jnp.int32, (BW, BW), 0) == lax.broadcasted_iota(
+        jnp.int32, (BW, BW), 1
+    )
+    wide[...] = steps_ref[...].astype(jnp.float32)
+    for a in range(2):
+
+        @pl.loop(0, 4 * half)
+        def _(i):
+            rows = pl.ds(pl.multiple_of(a * half * BW + i * (BW // 4), BW // 4), BW // 4)
+            total[rows, :] = jnp.zeros((BW // 4, cap * BW), jnp.float32)
+
+        @pl.when(z == t)
+        def _():
+            for r in range(a * half, (a + 1) * half):
+                total[r * BW : (r + 1) * BW, r * BW : (r + 1) * BW] = jnp.where(
+                    on_diagonal, diag_ref[r : r + 1, :], 0.0
+                )
+
+        load(a).wait()
+
+        @pl.loop(0, n * n * held)
+        def _(i):
+            source, q = i // (n * held), i % (n * held)
+            s = ((q // held) * n + source) * held + q % held
+            row = lax.rem(blocks_ref[s, z + a * n], cap)
+            rows = pl.ds(pl.multiple_of(row * BW, BW), BW)
+            for b in range(2):
+                col = lax.rem(blocks_ref[s, t + b * n], cap)
+                cols = pl.ds(pl.multiple_of(col * BW, BW), BW)
+                total[rows, cols] += box[a, source, q, :, b * BW : (b + 1) * BW].astype(jnp.float32)
+
+        store(a).start()
+    for j in range(held):
+        mine = (z * n + t) * held + j
+        picked = jnp.concatenate(
+            [wide[pl.ds(blocks_ref[mine, k], 1), :] for k in range(2 * n)], axis=1
+        )
+        applied = lax.dot_general(
+            picked.astype(jnp.bfloat16),
+            linking_ref[j],
+            (((1,), (1,)), ((), ())),
+            preferred_element_type=jnp.float32,
+        )
+        back_ref[j : j + 1, :] = scaling_ref[j : j + 1, :] * (residual_ref[j : j + 1, :] - applied)
+    store(0).wait()
+    store(1).wait()
+
+
+def assemble(n, blocks, got, first_diag, steps, linking, scaling, residual):
+    held = linking.shape[0]
+    cap = first_diag.shape[0] // BW
+    vmem = pl.BlockSpec(memory_space=pltpu.VMEM)
+    anywhere = pl.BlockSpec(memory_space=pl.ANY)
+    return pl.pallas_call(
+        functools.partial(assemble_kernel, n, held, cap),
+        out_shape=(
+            jax.ShapeDtypeStruct((cap * BW, cap * BW), jnp.float32),
+            jax.ShapeDtypeStruct(scaling.shape, jnp.float32),
+        ),
+        in_specs=[
+            pl.BlockSpec(memory_space=pltpu.SMEM), anywhere, vmem, vmem, vmem, vmem, vmem,
+        ],
+        out_specs=(anywhere, vmem),
+        scratch_shapes=[
+            pltpu.VMEM((2, n, n * held, BW, 2 * BW), jnp.bfloat16),
+            pltpu.VMEM((cap * BW, cap * BW), jnp.float32),
+            pltpu.VMEM(steps.shape, jnp.float32),
+            pltpu.SemaphoreType.DMA((2,)),
+            pltpu.SemaphoreType.DMA((2,)),
+        ],
+        compiler_params=pltpu.CompilerParams(vmem_limit_bytes=40 * 2**20),
+        name="assemble",
+    )(blocks, got, first_diag.reshape(cap, BW), steps, linking, scaling, residual)
+
+
+def on_square(linking, scaling, residual, blocks, step_dx, first_diag):
+    n = lax.axis_size("tile")
+    scaled = (jnp.sqrt(scaling)[:, :, None] * linking).astype(jnp.bfloat16)
+    got, steps = exchange(n, scaled, step_dx)
+    return assemble(n, blocks, got, first_diag, steps, linking, scaling, residual)
+
+
 def solution(mesh):
     in_specs = (
         P(("groups", "scen", "tile"), None, None),
@@ -103,6 +415,8 @@
         P(("groups", "scen")),
     )
     out_specs = (P(("groups", "scen"), "tile"), P(("groups", "scen", "tile"), None))
+    tiles_ax, scen_ax = mesh.shape["tile"], mesh.shape["scen"]
+    square = scen_ax == tiles_ax and LIST == 2 * tiles_ax
     return jax.shard_map(
-        on_device, mesh=mesh, in_specs=in_specs, out_specs=out_specs, check_vma=False
-    )
+        on_square if square else on_device, mesh=mesh, in_specs=in_specs, out_specs=out_specs, check_vma=False
+    )

time: 236 us -> 95.2 us (0.40)
  waiting for transfers between devices: 138 us -> 0 us
  Pallas kernels: 0 us -> 90.5 us
  local copies, waits for them, and re-layouts: 49.5 us -> 1.56 us
  blocking collectives: 14.8 us -> 0 us
  other arithmetic: 12.8 us -> 1.46 us
  starting transfers between devices: 10 us -> 0 us
  matrix products: 9.49 us -> 0 us
    all_to_all x2 -> x0, waiting for transfers between devices: 138 us -> none  [the longest x1 90.8 us: on_device(): lax.all_to_all(outbox, 'scen', split_axis=0, concat_axis=0, tiled=True)]
    pallas_call x0 -> x2, Pallas kernels: none -> 90.5 us  [the longest x1 80.5 us: exchange(): pl.pallas_call(functools.partial(exchange_kernel, n, held), out_shape=(ja...]
    scatter x1 -> x0, local copies, waits for them, and re-layouts: 20.7 us -> none  [on_device(): outbox = jnp.zeros((scen_ax, slot_count, BW, BW), jnp.bfloat16).at[send_o...]
    all_gather x1 -> x0, blocking collectives: 14.8 us -> none  [on_device(): full_step = lax.all_gather(low_step, 'scen', axis=0, tiled=True)]
    all_to_all x2 -> x0, starting transfers between devices: 10 us -> none  [the longest x1 5.04 us: on_device(): lax.all_to_all(outbox, 'scen', split_axis=0, concat_axis=0, tiled=True)]
    dot_general x4 -> x0, matrix products: 9.49 us -> none  [the longest x1 4.54 us: on_device(): jnp.dot(select, received.reshape(scen_ax * slot_count, BW * BW), preferre...]
    add x3 -> x0, other arithmetic: 8.84 us -> none  [the longest x1 8.76 us: on_device(): schur_block + jnp.where(rows_global[:, None] == cols_global[None, :], fir...]
    unnamed x6 -> x11, local copies, waits for them, and re-layouts: 8.84 us -> 0.79 us
  transfers between devices with their start and end apart: 2 -> 0, of which waited for: 2 -> 0; matrix products, arithmetic and copies ran while one was open for 1% -> 0% of each run, Pallas kernels for 0% -> 0%
where the time goes in v1:
time: 95.2 us; the launch traced here: 94.2 us
  Pallas kernels  90.5 us (95%)
  local copies, waits for them, and re-layouts  1.56 us (2%)
  other arithmetic  1.46 us (2%)
    pallas_call x1, Pallas kernels, exchange(): pl.pallas_call(functools.partial(exchange_kernel, n, held), out_shape=(ja...  80.5 us
    pallas_call x1, Pallas kernels, assemble(): pl.pallas_call(functools.partial(assemble_kernel, n, held, cap), out_shap...  9.99 us

profile of v1, /device:TPU:0, one launch (start us, length us, event | category | flops | bytes accessed | tf_op | source)
XLA Modules:
  0.0 94.2 jit_solution(4042954519705326705)
XLA Ops:
  0.6 0.0 copy-start.3
  0.6 0.0 copy-start
  0.7 0.0 copy-start.2
  0.7 0.0 copy-start.1
  0.7 0.0 copy-start.4
  0.7 0.8 sqrt.3
  1.5 0.8 copy.8.blocks_ref
  2.2 1.5 %multiply_convert_fusion.scaled_ref = bf16[2,256,1024]{2,1,0:T(8,128)(2,1)S(1)} fusion(bf16[2,256,1024]{2,1,0:T(8,128)(2,1)} %linking_ref.1, f32[2,256]{1,0:T(2,128)S(1)} %sqrt.3), kind=kLoop, calls=%fused_computation | loop fusion | flops 1572864 | bytes 2099200 | tf_op jit(solution)/shard_map/convert_element_type | solution.py:403
  3.7 0.0 copy-done.1
  3.7 80.5 %exchange.1 = (bf16[4,8,256,256]{3,2,1,0:T(8,128)(2,1)S(1)}, bf16[64,128]{1,0:T(8,128)(2,1)S(1)}) custom-call(bf16[2,256,1024]{2,1,0:T(8,128)(2,1)S(1)} %multiply_convert_fusion.scaled_ref, f32[16,128]{1,0:T(8,128)S(1)} %copy-done.1), custom_call_target="tpu_custom_call" | custom-call | tf_op jit(solution)/shard_map/exchange/pallas_call | solution.py:278
  84.2 0.0 copy-done.3
  84.2 0.0 copy-done
  84.2 0.0 copy-done.2
  84.2 0.0 copy-done.4
  84.2 10.0 %assemble.1 = (f32[2048,2048]{1,0:T(8,128)}, f32[2,256]{1,0:T(2,128)}) custom-call(s32[32,8]{1,0:T(8,128)S(1)} %copy.8.blocks_ref, bf16[4,8,256,256]{3,2,1,0:T(8,128)(2,1)S(1)} %get-tuple-element.4.got_ref, f32[16,128]{1,0:T(8,128)S(1)} %bitcast.1, bf16[64,128]{1,0:T(8,128)(2,1)S(1)} %get-tuple-element.5.steps_ref, bf16[2,256,1024]{2,1,0:T(8,128)(2,1)S(1)} %copy-done, ...), custom_call_target="tpu_custom_call" | custom-call | tf_op jit(solution)/shard_map/assemble/pallas_call | solution.py:379
Async XLA Ops:
  0.6 83.6 %copy-start.3 = (f32[2,256]{1,0:T(2,128)S(1)}, f32[2,256]{1,0:T(2,128)}, u32[]{:S(2)}) copy-start(f32[2,256]{1,0:T(2,128)} %scaling_ref.1) | copy-start | bytes 6148
  0.6 83.6 %copy-start = (bf16[2,256,1024]{2,1,0:T(8,128)(2,1)S(1)}, bf16[2,256,1024]{2,1,0:T(8,128)(2,1)}, u32[]{:S(2)}) copy-start(bf16[2,256,1024]{2,1,0:T(8,128)(2,1)} %linking_ref.1) | copy-start | bytes 3145732
  0.7 83.6 %copy-start.2 = (f32[2048]{0:T(1024)S(1)}, f32[2048]{0:T(1024)}, u32[]{:S(2)}) copy-start(f32[2048]{0:T(1024)} %param.11) | copy-start | bytes 24580
  0.7 3.0 %copy-start.1 = (f32[16,128]{1,0:T(8,128)S(1)}, f32[16,128]{1,0:T(8,128)}, u32[]{:S(2)}) copy-start(f32[16,128]{1,0:T(8,128)} %step_ref.1) | copy-start | bytes 24580
  0.7 83.6 %copy-start.4 = (f32[2,256]{1,0:T(2,128)S(1)}, f32[2,256]{1,0:T(2,128)}, u32[]{:S(2)}) copy-start(f32[2,256]{1,0:T(2,128)} %residual_ref.1) | copy-start | bytes 6148

commit v2 on v0

--- a/solution.py
+++ b/solution.py
@@ -1,6 +1,10 @@
+import functools
+
 import jax
 import jax.numpy as jnp
 from jax import lax
+from jax.experimental import pallas as pl
+from jax.experimental.pallas import tpu as pltpu
 from jax.sharding import PartitionSpec as P
 
 BW = 128
@@ -93,6 +97,389 @@
     return (schur_block, back_step)
 
 
+MESH = pl.DeviceIdType.MESH
+PACK = BW + 16
+
+
+def pair_masks():
+    rows = lax.broadcasted_iota(jnp.int32, (BW, BW), 0)
+    cols = lax.broadcasted_iota(jnp.int32, (BW, BW), 1)
+    return rows > cols, rows == cols, rows < cols
+
+
+def exchange_kernel(
+    n, held, linking_ref, scaling_ref, step_ref, got_ref, steps_ref,
+    gathered, parts, end_parts, step_box,
+    own_sem, pass_sem, chain_sem, end_sem, end_got_sem, part_sem, got_sem, keep_sem,
+    step_sem, step_got_sem,
+):
+    z = lax.axis_index("scen")
+    t = lax.axis_index("tile")
+    side = z // (n // 2)
+    end = side * (n - 1)
+    turn = 1 - 2 * side
+    inner = (z > 0) & (z < n - 1)
+    peers = (lax.rem(t + 2, n), n - 1 - t, t + 1 - 2 * lax.rem(t, 2))
+    below, level, above = pair_masks()
+
+    def is_inner(place):
+        return (place > 0) & (place < n - 1)
+
+    def hop(source, j, sem, to):
+        return pltpu.make_async_remote_copy(
+            src_ref=gathered.at[source, j],
+            dst_ref=gathered.at[source, j],
+            send_sem=sem,
+            recv_sem=chain_sem.at[source, j],
+            device_id={"scen": to},
+            device_id_type=MESH,
+        )
+
+    def by_size(packed, act):
+        @pl.when(packed)
+        def _():
+            act(PACK)
+
+        @pl.when(jnp.logical_not(packed))
+        def _():
+            act(2 * BW)
+
+    def end_send(q, to, size):
+        return pltpu.make_async_remote_copy(
+            src_ref=end_parts.at[q, to, pl.ds(0, size)],
+            dst_ref=parts.at[q, to, pl.ds(0, size)],
+            send_sem=end_sem.at[q, to],
+            recv_sem=end_got_sem.at[q, to],
+            device_id={"scen": end},
+            device_id_type=MESH,
+        )
+
+    def part_send(q, to, size):
+        return pltpu.make_async_remote_copy(
+            src_ref=parts.at[q, to, pl.ds(0, size)],
+            dst_ref=got_ref.at[t, q, pl.ds(0, size)],
+            send_sem=part_sem.at[q, to],
+            recv_sem=got_sem.at[t, q],
+            device_id={"tile": to},
+            device_id_type=MESH,
+        )
+
+    def part_arrival(source, q, size):
+        return pltpu.make_async_remote_copy(
+            src_ref=parts.at[q, source, pl.ds(0, size)],
+            dst_ref=got_ref.at[source, q, pl.ds(0, size)],
+            send_sem=part_sem.at[q, source],
+            recv_sem=got_sem.at[source, q],
+            device_id={"tile": source},
+            device_id_type=MESH,
+        )
+
+    def part_keep(q, size):
+        return pltpu.make_async_copy(
+            parts.at[q, t, pl.ds(0, size)], got_ref.at[t, q, pl.ds(0, size)], keep_sem.at[q]
+        )
+
+    def step_copy(place, to, d):
+        return pltpu.make_async_remote_copy(
+            src_ref=step_box.at[place],
+            dst_ref=step_box.at[place],
+            send_sem=step_sem.at[d - 1],
+            recv_sem=step_got_sem.at[place],
+            device_id={"scen": to},
+            device_id_type=MESH,
+        )
+
+    def gram(dest, source, j, out):
+        q = source * held + j
+        block = gathered.at[source, j]
+        left = jnp.concatenate(
+            [block[:, pl.ds(pl.multiple_of((dest + a * n) * BW, BW), BW)] for a in range(2)],
+            axis=1,
+        )
+        turned = left.T
+        for to in range(n):
+            right = jnp.concatenate(
+                [block[:, (to + b * n) * BW : (to + b * n + 1) * BW] for b in range(2)], axis=1
+            )
+            tiles = jnp.dot(turned, right, preferred_element_type=jnp.float32)
+
+            @pl.when(dest != to)
+            def _():
+                out[q, to] = tiles.astype(jnp.bfloat16)
+
+            @pl.when(dest == to)
+            def _():
+                first, cross, second = tiles[:BW, :BW], tiles[:BW, BW:], tiles[BW:, BW:]
+                out[q, to, :BW, :BW] = jnp.where(above, second, first).astype(jnp.bfloat16)
+                out[q, to, :BW, BW:] = cross.astype(jnp.bfloat16)
+                line = jnp.sum(jnp.where(level, second, 0.0), axis=0, keepdims=True)
+                out[q, to, BW:PACK, :BW] = jnp.broadcast_to(line, (PACK - BW, BW)).astype(
+                    jnp.bfloat16
+                )
+
+    def unpack(source, q):
+        mixed = got_ref[source, q, :BW, :BW].astype(jnp.float32)
+        cross = got_ref[source, q, :BW, BW:].astype(jnp.float32)
+        line = got_ref[source, q, BW:PACK, :BW].astype(jnp.float32)[:1]
+        flipped = mixed.T
+        first = jnp.where(above, flipped, mixed)
+        second = jnp.where(above, mixed, jnp.where(below, flipped, line))
+        got_ref[source, q, :BW, :BW] = first.astype(jnp.bfloat16)
+        got_ref[source, q, BW:, :BW] = cross.T.astype(jnp.bfloat16)
+        got_ref[source, q, BW:, BW:] = second.astype(jnp.bfloat16)
+
+    def to_end(source, j):
+        q = source * held + j
+        gram(end, source, j, end_parts)
+        for to in peers + (t,):
+            by_size(to == end, lambda size: end_send(q, to, size).start())
+
+    def to_plane(source, j):
+        q = source * held + j
+        gram(z, source, j, parts)
+        for to in peers:
+            by_size(to == z, lambda size: part_send(q, to, size).start())
+        by_size(t == z, lambda size: part_keep(q, size).start())
+
+    barrier = pltpu.get_barrier_semaphore()
+    for d in range(1, n):
+        pl.semaphore_signal(
+            barrier, inc=1, device_id={"scen": lax.rem(z + d, n)}, device_id_type=MESH
+        )
+        pl.semaphore_signal(
+            barrier, inc=1, device_id={"tile": lax.rem(t + d, n)}, device_id_type=MESH
+        )
+    step_box[z] = step_ref[...].astype(jnp.bfloat16)
+    rows = linking_ref.shape[1]
+    diagonal = lax.broadcasted_iota(jnp.int32, (rows, rows), 0) == lax.broadcasted_iota(
+        jnp.int32, (rows, rows), 1
+    )
+    for j in range(held):
+        root = jnp.sqrt(scaling_ref[j : j + 1, :])
+        column = jnp.sum(jnp.where(diagonal, root, 0.0), axis=1, keepdims=True)
+        gathered[z, j] = (column * linking_ref[j].astype(jnp.float32)).astype(jnp.bfloat16)
+    pl.semaphore_wait(barrier, 2 * (n - 1))
+
+    @pl.loop(0, held)
+    def _(j):
+        for way in (1, -1):
+
+            @pl.when(is_inner(z + way))
+            def _():
+                hop(z, j, own_sem.at[(1 - way) // 2, j], z + way).start()
+
+        @pl.when(inner)
+        def _():
+            to_end(z, j)
+
+    for d in range(1, n):
+        step_copy(z, lax.rem(z + d, n), d).start()
+
+    @pl.loop(0, held)
+    def _(j):
+        to_plane(z, j)
+
+    @pl.when(inner)
+    def _():
+        @pl.loop(0, 2 * held * (n - 2))
+        def _(i):
+            d = 1 + i // (2 * held)
+            j = (i // 2) % held
+            way = 1 - 2 * (i % 2)
+            source = z - way * d
+            onward = z + way
+
+            @pl.when((source >= 0) & (source < n))
+            def _():
+                hop(source, j, pass_sem.at[source, j], z).wait_recv()
+
+                @pl.when(is_inner(onward))
+                def _():
+                    hop(source, j, pass_sem.at[source, j], onward).start()
+
+                @pl.when(jnp.logical_not(is_inner(onward)))
+                def _():
+                    to_end(source, j)
+
+                to_plane(source, j)
+
+    @pl.when(jnp.logical_not(inner))
+    def _():
+        @pl.loop(0, held * (n - 1))
+        def _(i):
+            q = (z + turn * (1 + i // held)) * held + i % held
+            for to in peers:
+                by_size(to == z, lambda size: end_send(q, to, size).wait_recv())
+                by_size(to == z, lambda size: part_send(q, to, size).start())
+            by_size(t == z, lambda size: end_send(q, t, size).wait_recv())
+            by_size(t == z, lambda size: part_keep(q, size).start())
+
+    for d in range(1, n):
+        step_copy(z, lax.rem(z + d, n), d).wait_send()
+        source = lax.rem(z + d, n)
+        step_copy(source, source, d).wait_recv()
+    steps_ref[...] = step_box[...].reshape(steps_ref.shape)
+
+    @pl.loop(0, held)
+    def _(j):
+        for way in (1, -1):
+
+            @pl.when(is_inner(z + way))
+            def _():
+                hop(z, j, own_sem.at[(1 - way) // 2, j], z + way).wait_send()
+
+    @pl.when(inner)
+    def _():
+        @pl.loop(0, held)
+        def _(j):
+            hop(end, j, pass_sem.at[end, j], z + turn).wait_send()
+
+        @pl.loop(0, held * (n - 1))
+        def _(i):
+            q = (end + turn * (1 + i // held)) * held + i % held
+            for to in range(n):
+                by_size(to == end, lambda size: end_send(q, to, size).wait_send())
+
+    @pl.loop(0, n * held)
+    def _(i):
+        q = lax.rem(z + turn * (i // held) + n, n) * held + i % held
+        by_size(t == z, lambda size: part_keep(q, size).wait())
+        for to in peers:
+            by_size(t == z, lambda size: part_arrival(to, q, size).wait_recv())
+
+        @pl.when(t == z)
+        def _():
+            for source in range(n):
+                unpack(source, q)
+
+        for to in peers:
+            by_size(to == z, lambda size: part_send(q, to, size).wait_send())
+
+
+def exchange(n, linking, scaling, step_dx):
+    held, rows, width = linking.shape
+    vmem = pl.BlockSpec(memory_space=pltpu.VMEM)
+    return pl.pallas_call(
+        functools.partial(exchange_kernel, n, held),
+        out_shape=(
+            jax.ShapeDtypeStruct((n, n * held, 2 * BW, 2 * BW), jnp.bfloat16),
+            jax.ShapeDtypeStruct((n * step_dx.shape[0], BW), jnp.bfloat16),
+        ),
+        in_specs=[vmem] * 3,
+        out_specs=(vmem, vmem),
+        scratch_shapes=[
+            pltpu.VMEM((n, held, rows, width), jnp.bfloat16),
+            pltpu.VMEM((n * held, n, 2 * BW, 2 * BW), jnp.bfloat16),
+            pltpu.VMEM((n * held, n, 2 * BW, 2 * BW), jnp.bfloat16),
+            pltpu.VMEM((n,) + step_dx.shape, jnp.bfloat16),
+            pltpu.SemaphoreType.DMA((2, held)),
+            pltpu.SemaphoreType.DMA((n, held)),
+            pltpu.SemaphoreType.DMA((n, held)),
+            pltpu.SemaphoreType.DMA((n * held, n)),
+            pltpu.SemaphoreType.DMA((n * held, n)),
+            pltpu.SemaphoreType.DMA((n * held, n)),
+            pltpu.SemaphoreType.DMA((n, n * held)),
+            pltpu.SemaphoreType.DMA((n * held,)),
+            pltpu.SemaphoreType.DMA((n - 1,)),
+            pltpu.SemaphoreType.DMA((n,)),
+        ],
+        compiler_params=pltpu.CompilerParams(
+            collective_id=0, has_side_effects=True, vmem_limit_bytes=36 * 2**20
+        ),
+        name="exchange",
+    )(linking, scaling, step_dx)
+
+
+def assemble_kernel(
+    n, held, cap, lists_ref, got_ref, diag_ref, steps_ref, linking_ref, scaling_ref, residual_ref,
+    schur_ref, back_ref, total, wide, out_sem,
+):
+    z = lax.axis_index("scen")
+    t = lax.axis_index("tile")
+    half = cap // 2
+    span = half * BW
+
+    def store(a, b):
+        place = (pl.ds(a * span, span), pl.ds(b * span, span))
+        return pltpu.make_async_copy(total.at[place], schur_ref.at[place], out_sem.at[a, b])
+
+    level = pair_masks()[1]
+    for a in range(2):
+        for b in range(2):
+
+            @pl.loop(0, 2 * half)
+            def _(i):
+                rows = pl.ds(pl.multiple_of(a * span + i * (BW // 2), BW // 2), BW // 2)
+                total[rows, b * span : (b + 1) * span] = jnp.zeros((BW // 2, span), jnp.float32)
+
+            if a == b:
+
+                @pl.when(z == t)
+                def _():
+                    for r in range(a * half, (a + 1) * half):
+                        total[r * BW : (r + 1) * BW, r * BW : (r + 1) * BW] = jnp.where(
+                            level, diag_ref[r : r + 1, :], 0.0
+                        )
+
+            @pl.loop(0, n * n * held, unroll=4)
+            def _(i):
+                source, q = i // (n * held), i % (n * held)
+                s = ((q // held) * n + source) * held + q % held
+                row = lax.rem(lists_ref[z + a * n, s], cap)
+                col = lax.rem(lists_ref[t + b * n, s], cap)
+                rows = pl.ds(pl.multiple_of(row * BW, BW), BW)
+                cols = pl.ds(pl.multiple_of(col * BW, BW), BW)
+                total[rows, cols] += got_ref[
+                    source, q, a * BW : (a + 1) * BW, b * BW : (b + 1) * BW
+                ].astype(jnp.float32)
+
+            store(a, b).start()
+    wide[...] = steps_ref[...].astype(jnp.float32)
+    for j in range(held):
+        mine = (z * n + t) * held + j
+        picked = jnp.concatenate(
+            [wide[pl.ds(lists_ref[k, mine], 1), :] for k in range(2 * n)], axis=1
+        )
+        applied = lax.dot_general(
+            picked.astype(jnp.bfloat16),
+            linking_ref[j],
+            (((1,), (1,)), ((), ())),
+            preferred_element_type=jnp.float32,
+        )
+        back_ref[j : j + 1, :] = scaling_ref[j : j + 1, :] * (residual_ref[j : j + 1, :] - applied)
+    for a in range(2):
+        for b in range(2):
+            store(a, b).wait()
+
+
+def assemble(n, lists, got, first_diag, steps, linking, scaling, residual):
+    held = linking.shape[0]
+    cap = first_diag.shape[0] // BW
+    vmem = pl.BlockSpec(memory_space=pltpu.VMEM)
+    return pl.pallas_call(
+        functools.partial(assemble_kernel, n, held, cap),
+        out_shape=(
+            jax.ShapeDtypeStruct((cap * BW, cap * BW), jnp.float32),
+            jax.ShapeDtypeStruct(scaling.shape, jnp.float32),
+        ),
+        in_specs=[pl.BlockSpec(memory_space=pltpu.SMEM)] + [vmem] * 6,
+        out_specs=(pl.BlockSpec(memory_space=pl.ANY), vmem),
+        scratch_shapes=[
+            pltpu.VMEM((cap * BW, cap * BW), jnp.float32),
+            pltpu.VMEM(steps.shape, jnp.float32),
+            pltpu.SemaphoreType.DMA((2, 2)),
+        ],
+        compiler_params=pltpu.CompilerParams(vmem_limit_bytes=36 * 2**20),
+        name="assemble",
+    )(lists, got, first_diag.reshape(cap, BW), steps, linking, scaling, residual)
+
+
+def on_square(linking, scaling, residual, blocks, step_dx, first_diag):
+    n = lax.axis_size("tile")
+    got, steps = exchange(n, linking, scaling, step_dx)
+    return assemble(n, blocks.T, got, first_diag, steps, linking, scaling, residual)
+
+
 def solution(mesh):
     in_specs = (
         P(("groups", "scen", "tile"), None, None),
@@ -103,6 +490,8 @@
         P(("groups", "scen")),
     )
     out_specs = (P(("groups", "scen"), "tile"), P(("groups", "scen", "tile"), None))
+    tiles_ax, scen_ax = mesh.shape["tile"], mesh.shape["scen"]
+    square = scen_ax == tiles_ax and LIST == 2 * tiles_ax
     return jax.shard_map(
-        on_device, mesh=mesh, in_specs=in_specs, out_specs=out_specs, check_vma=False
-    )
+        on_square if square else on_device, mesh=mesh, in_specs=in_specs, out_specs=out_specs, check_vma=False
+    )

time: 236 us -> 84.5 us (0.36)
  waiting for transfers between devices: 138 us -> 0 us
  Pallas kernels: 0 us -> 78.9 us
  local copies, waits for them, and re-layouts: 49.5 us -> 4.65 us
  blocking collectives: 14.8 us -> 0 us
  other arithmetic: 12.8 us -> 0 us
  starting transfers between devices: 10 us -> 0 us
  matrix products: 9.49 us -> 0 us
    all_to_all x2 -> x0, waiting for transfers between devices: 138 us -> none  [the longest x1 90.8 us: on_device(): lax.all_to_all(outbox, 'scen', split_axis=0, concat_axis=0, tiled=True)]
    pallas_call x0 -> x2, Pallas kernels: none -> 78.9 us  [the longest x1 70.6 us: exchange(): pl.pallas_call(functools.partial(exchange_kernel, n, held), out_shape=(ja...]
    scatter x1 -> x0, local copies, waits for them, and re-layouts: 20.7 us -> none  [on_device(): outbox = jnp.zeros((scen_ax, slot_count, BW, BW), jnp.bfloat16).at[send_o...]
    all_gather x1 -> x0, blocking collectives: 14.8 us -> none  [on_device(): full_step = lax.all_gather(low_step, 'scen', axis=0, tiled=True)]
    all_to_all x2 -> x0, starting transfers between devices: 10 us -> none  [the longest x1 5.04 us: on_device(): lax.all_to_all(outbox, 'scen', split_axis=0, concat_axis=0, tiled=True)]
    dot_general x4 -> x0, matrix products: 9.49 us -> none  [the longest x1 4.54 us: on_device(): jnp.dot(select, received.reshape(scen_ax * slot_count, BW * BW), preferre...]
    add x3 -> x0, other arithmetic: 8.84 us -> none  [the longest x1 8.76 us: on_device(): schur_block + jnp.where(rows_global[:, None] == cols_global[None, :], fir...]
    dot_general x1 -> x0, local copies, waits for them, and re-layouts: 6.39 us -> none  [on_device(): jnp.dot(select, received.reshape(scen_ax * slot_count, BW * BW), preferre...]
  transfers between devices with their start and end apart: 2 -> 0, of which waited for: 2 -> 0; matrix products, arithmetic and copies ran while one was open for 1% -> 0% of each run, Pallas kernels for 0% -> 0%
where the time goes in v2:
time: 84.5 us; the launch traced here: 84.2 us
  Pallas kernels  78.9 us (93%)
  local copies, waits for them, and re-layouts  4.65 us (6%)
    pallas_call x1, Pallas kernels, exchange(): pl.pallas_call(functools.partial(exchange_kernel, n, held), out_shape=(ja...  70.6 us
    pallas_call x1, Pallas kernels, assemble(): pl.pallas_call(functools.partial(assemble_kernel, n, held, cap), out_shap...  8.26 us
    unnamed x12, local copies, waits for them, and re-layouts  4.65 us

profile of v2, /device:TPU:0, one launch (start us, length us, event | category | flops | bytes accessed | tf_op | source)
XLA Modules:
  0.0 84.2 jit_solution(5397335246178550029)
XLA Ops:
  0.6 0.0 copy-start
  0.6 1.2 %copy-done = bf16[2,256,1024]{2,1,0:T(8,128)(2,1)S(1)} copy-done((bf16[2,256,1024]{2,1,0:T(8,128)(2,1)S(1)}, bf16[2,256,1024]{2,1,0:T(8,128)(2,1)}, u32[]{:S(2)}) %copy-start) | copy-done | bytes 1048600
  1.9 0.0 copy-start.1
  1.9 0.7 copy-done.1
  2.5 0.0 copy-start.2
  2.5 0.7 copy-done.2
  3.2 70.6 %exchange.1 = (bf16[4,8,256,256]{3,2,1,0:T(8,128)(2,1)S(1)}, bf16[64,128]{1,0:T(8,128)(2,1)S(1)}) custom-call(bf16[2,256,1024]{2,1,0:T(8,128)(2,1)S(1)} %copy-done, f32[2,256]{1,0:T(2,128)S(1)} %copy-done.1, f32[16,128]{1,0:T(8,128)S(1)} %copy-done.2), custom_call_target="tpu_custom_call" | custom-call | tf_op jit(solution)/shard_map/exchange/pallas_call | solution.py:362
  73.9 0.0 copy-start.3
  73.9 0.7 copy-done.3
  74.6 0.0 copy-start.4
  74.6 0.7 copy-done.4
  75.3 0.0 copy-start.5
  75.3 0.7 copy-done.5
  75.9 8.3 %assemble.1 = (f32[2048,2048]{1,0:T(8,128)}, f32[2,256]{1,0:T(2,128)}) custom-call(s32[8,32]{1,0:T(8,128)S(1)} %bitcast.3, bf16[4,8,256,256]{3,2,1,0:T(8,128)(2,1)S(1)} %get-tuple-element.4.got_ref, f32[16,128]{1,0:T(8,128)S(1)} %bitcast.2, bf16[64,128]{1,0:T(8,128)(2,1)S(1)} %get-tuple-element.5.steps_ref, bf16[2,256,1024]{2,1,0:T(8,128)(2,1)S(1)} %copy-done, ...), custom_call_target="tpu_custom_call" | custom-call | tf_op jit(solution)/shard_map/assemble/pallas_call | solution.py:459
Async XLA Ops:
  0.6 1.2 %copy-start = (bf16[2,256,1024]{2,1,0:T(8,128)(2,1)S(1)}, bf16[2,256,1024]{2,1,0:T(8,128)(2,1)}, u32[]{:S(2)}) copy-start(bf16[2,256,1024]{2,1,0:T(8,128)(2,1)} %linking_ref.3) | copy-start | bytes 3145732
  1.9 0.7 copy-start.1
  2.5 0.7 copy-start.2
  73.9 0.7 copy-start.3
  74.6 0.7 copy-start.4
  75.3 0.7 copy-start.5

commit v3 on v2

--- a/solution.py
+++ b/solution.py
@@ -108,9 +108,9 @@
 
 
 def exchange_kernel(
-    n, held, linking_ref, scaling_ref, step_ref, got_ref, steps_ref,
+    n, held, scaled_ref, step_ref, got_ref, steps_ref,
     gathered, parts, end_parts, step_box,
-    own_sem, pass_sem, chain_sem, end_sem, end_got_sem, part_sem, got_sem, keep_sem,
+    load_sem, own_sem, pass_sem, chain_sem, end_sem, end_got_sem, part_sem, got_sem, keep_sem,
     step_sem, step_got_sem,
 ):
     z = lax.axis_index("scen")
@@ -189,7 +189,7 @@
             device_id_type=MESH,
         )
 
-    def gram(dest, source, j, out):
+    def gram(dest, source, j, out, send):
         q = source * held + j
         block = gathered.at[source, j]
         left = jnp.concatenate(
@@ -197,9 +197,13 @@
             axis=1,
         )
         turned = left.T
-        for to in range(n):
+        for to in peers + (t,):
             right = jnp.concatenate(
-                [block[:, (to + b * n) * BW : (to + b * n + 1) * BW] for b in range(2)], axis=1
+                [
+                    block[:, pl.ds(pl.multiple_of((to + b * n) * BW, BW), BW)]
+                    for b in range(2)
+                ],
+                axis=1,
             )
             tiles = jnp.dot(turned, right, preferred_element_type=jnp.float32)
 
@@ -216,6 +220,8 @@
                 out[q, to, BW:PACK, :BW] = jnp.broadcast_to(line, (PACK - BW, BW)).astype(
                     jnp.bfloat16
                 )
+
+            send(q, to)
 
     def unpack(source, q):
         mixed = got_ref[source, q, :BW, :BW].astype(jnp.float32)
@@ -229,18 +235,37 @@
         got_ref[source, q, BW:, BW:] = second.astype(jnp.bfloat16)
 
     def to_end(source, j):
-        q = source * held + j
-        gram(end, source, j, end_parts)
-        for to in peers + (t,):
+        def send(q, to):
             by_size(to == end, lambda size: end_send(q, to, size).start())
 
+        gram(end, source, j, end_parts, send)
+
+    def pass_on(q, to):
+        if to is t:
+            by_size(t == z, lambda size: part_keep(q, size).start())
+        else:
+            by_size(to == z, lambda size: part_send(q, to, size).start())
+
     def to_plane(source, j):
-        q = source * held + j
-        gram(z, source, j, parts)
+        gram(z, source, j, parts, pass_on)
+
+    def finish(p):
+        q = lax.rem(z + turn * (p // held) + n, n) * held + p % held
+        by_size(t == z, lambda size: part_keep(q, size).wait())
         for to in peers:
-            by_size(to == z, lambda size: part_send(q, to, size).start())
-        by_size(t == z, lambda size: part_keep(q, size).start())
-
+            by_size(t == z, lambda size: part_arrival(to, q, size).wait_recv())
+
+        @pl.when(t == z)
+        def _():
+            for source in range(n):
+                unpack(source, q)
+
+    loads = [
+        pltpu.make_async_copy(scaled_ref.at[j], gathered.at[z, j], load_sem.at[j])
+        for j in range(held)
+    ]
+    for load in loads:
+        load.start()
     barrier = pltpu.get_barrier_semaphore()
     for d in range(1, n):
         pl.semaphore_signal(
@@ -250,14 +275,8 @@
             barrier, inc=1, device_id={"tile": lax.rem(t + d, n)}, device_id_type=MESH
         )
     step_box[z] = step_ref[...].astype(jnp.bfloat16)
-    rows = linking_ref.shape[1]
-    diagonal = lax.broadcasted_iota(jnp.int32, (rows, rows), 0) == lax.broadcasted_iota(
-        jnp.int32, (rows, rows), 1
-    )
-    for j in range(held):
-        root = jnp.sqrt(scaling_ref[j : j + 1, :])
-        column = jnp.sum(jnp.where(diagonal, root, 0.0), axis=1, keepdims=True)
-        gathered[z, j] = (column * linking_ref[j].astype(jnp.float32)).astype(jnp.bfloat16)
+    for load in loads:
+        load.wait()
     pl.semaphore_wait(barrier, 2 * (n - 1))
 
     @pl.loop(0, held)
@@ -308,11 +327,10 @@
         @pl.loop(0, held * (n - 1))
         def _(i):
             q = (z + turn * (1 + i // held)) * held + i % held
-            for to in peers:
+            for to in peers + (t,):
                 by_size(to == z, lambda size: end_send(q, to, size).wait_recv())
-                by_size(to == z, lambda size: part_send(q, to, size).start())
-            by_size(t == z, lambda size: end_send(q, t, size).wait_recv())
-            by_size(t == z, lambda size: part_keep(q, size).start())
+                pass_on(q, to)
+            finish(i)
 
     for d in range(1, n):
         step_copy(z, lax.rem(z + d, n), d).wait_send()
@@ -320,6 +338,16 @@
         step_copy(source, source, d).wait_recv()
     steps_ref[...] = step_box[...].reshape(steps_ref.shape)
 
+    @pl.when(inner)
+    def _():
+        @pl.loop(0, held * (n - 1))
+        def _(p):
+            finish(p)
+
+    @pl.loop(held * (n - 1), held * n)
+    def _(p):
+        finish(p)
+
     @pl.loop(0, held)
     def _(j):
         for way in (1, -1):
@@ -341,23 +369,13 @@
                 by_size(to == end, lambda size: end_send(q, to, size).wait_send())
 
     @pl.loop(0, n * held)
-    def _(i):
-        q = lax.rem(z + turn * (i // held) + n, n) * held + i % held
-        by_size(t == z, lambda size: part_keep(q, size).wait())
-        for to in peers:
-            by_size(t == z, lambda size: part_arrival(to, q, size).wait_recv())
-
-        @pl.when(t == z)
-        def _():
-            for source in range(n):
-                unpack(source, q)
-
+    def _(q):
         for to in peers:
             by_size(to == z, lambda size: part_send(q, to, size).wait_send())
 
 
-def exchange(n, linking, scaling, step_dx):
-    held, rows, width = linking.shape
+def exchange(n, scaled, step_dx):
+    held, rows, width = scaled.shape
     vmem = pl.BlockSpec(memory_space=pltpu.VMEM)
     return pl.pallas_call(
         functools.partial(exchange_kernel, n, held),
@@ -365,13 +383,14 @@
             jax.ShapeDtypeStruct((n, n * held, 2 * BW, 2 * BW), jnp.bfloat16),
             jax.ShapeDtypeStruct((n * step_dx.shape[0], BW), jnp.bfloat16),
         ),
-        in_specs=[vmem] * 3,
+        in_specs=[pl.BlockSpec(memory_space=pl.ANY), vmem],
         out_specs=(vmem, vmem),
         scratch_shapes=[
             pltpu.VMEM((n, held, rows, width), jnp.bfloat16),
             pltpu.VMEM((n * held, n, 2 * BW, 2 * BW), jnp.bfloat16),
             pltpu.VMEM((n * held, n, 2 * BW, 2 * BW), jnp.bfloat16),
             pltpu.VMEM((n,) + step_dx.shape, jnp.bfloat16),
+            pltpu.SemaphoreType.DMA((held,)),
             pltpu.SemaphoreType.DMA((2, held)),
             pltpu.SemaphoreType.DMA((n, held)),
             pltpu.SemaphoreType.DMA((n, held)),
@@ -384,57 +403,78 @@
             pltpu.SemaphoreType.DMA((n,)),
         ],
         compiler_params=pltpu.CompilerParams(
-            collective_id=0, has_side_effects=True, vmem_limit_bytes=36 * 2**20
+            collective_id=0, has_side_effects=True, vmem_limit_bytes=40 * 2**20
+        ),
+        cost_estimate=pl.CostEstimate(
+            flops=60_000_000_000, bytes_accessed=60_000_000_000 // 400, transcendentals=0
         ),
         name="exchange",
-    )(linking, scaling, step_dx)
+    )(scaled, step_dx)
 
 
 def assemble_kernel(
-    n, held, cap, lists_ref, got_ref, diag_ref, steps_ref, linking_ref, scaling_ref, residual_ref,
-    schur_ref, back_ref, total, wide, out_sem,
+    n, held, cap, lists_hbm, diag_hbm, linking_hbm, scaling_hbm, residual_hbm, got_ref, steps_ref,
+    schur_ref, back_ref, total, lists_ref, diag_ref, linking_ref, scaling_ref, residual_ref, wide,
+    load_sem, out_sem,
 ):
     z = lax.axis_index("scen")
     t = lax.axis_index("tile")
-    half = cap // 2
-    span = half * BW
-
-    def store(a, b):
-        place = (pl.ds(a * span, span), pl.ds(b * span, span))
-        return pltpu.make_async_copy(total.at[place], schur_ref.at[place], out_sem.at[a, b])
-
+    span = cap // 2 * BW
+
+    def store(a):
+        rows = pl.ds(a * span, span)
+        return pltpu.make_async_copy(total.at[rows], schur_ref.at[rows], out_sem.at[a])
+
+    pairs = (
+        (lists_hbm, lists_ref), (diag_hbm, diag_ref), (linking_hbm, linking_ref),
+        (scaling_hbm, scaling_ref), (residual_hbm, residual_ref),
+    )
+    loads = [
+        pltpu.make_async_copy(far, near, load_sem.at[k]) for k, (far, near) in enumerate(pairs)
+    ]
+    for load in loads:
+        load.start()
+    wide[...] = steps_ref[...].astype(jnp.float32)
     level = pair_masks()[1]
     for a in range(2):
-        for b in range(2):
-
-            @pl.loop(0, 2 * half)
-            def _(i):
-                rows = pl.ds(pl.multiple_of(a * span + i * (BW // 2), BW // 2), BW // 2)
-                total[rows, b * span : (b + 1) * span] = jnp.zeros((BW // 2, span), jnp.float32)
-
-            if a == b:
-
-                @pl.when(z == t)
-                def _():
-                    for r in range(a * half, (a + 1) * half):
-                        total[r * BW : (r + 1) * BW, r * BW : (r + 1) * BW] = jnp.where(
-                            level, diag_ref[r : r + 1, :], 0.0
-                        )
-
-            @pl.loop(0, n * n * held, unroll=4)
-            def _(i):
-                source, q = i // (n * held), i % (n * held)
-                s = ((q // held) * n + source) * held + q % held
-                row = lax.rem(lists_ref[z + a * n, s], cap)
-                col = lax.rem(lists_ref[t + b * n, s], cap)
-                rows = pl.ds(pl.multiple_of(row * BW, BW), BW)
-                cols = pl.ds(pl.multiple_of(col * BW, BW), BW)
-                total[rows, cols] += got_ref[
-                    source, q, a * BW : (a + 1) * BW, b * BW : (b + 1) * BW
-                ].astype(jnp.float32)
-
-            store(a, b).start()
-    wide[...] = steps_ref[...].astype(jnp.float32)
+
+        @pl.loop(0, span // 32)
+        def _(i):
+            rows = pl.ds(pl.multiple_of(a * span + i * 32, 32), 32)
+            total[rows, :] = jnp.zeros((32, cap * BW), jnp.float32)
+
+        if a == 0:
+            loads[0].wait()
+            loads[1].wait()
+
+        @pl.when(z == t)
+        def _():
+            for r in range(a * cap // 2, (a + 1) * cap // 2):
+                total[r * BW : (r + 1) * BW, r * BW : (r + 1) * BW] = jnp.where(
+                    level, diag_ref[r : r + 1, :], 0.0
+                )
+
+        @pl.loop(0, n * n * held, unroll=4)
+        def _(i):
+            source, q = i // (n * held), i % (n * held)
+            s = ((q // held) * n + source) * held + q % held
+            row = lists_ref[z + a * n, s] - z * cap
+            places, sums = [], []
+            for b in range(2):
+                col = lists_ref[t + b * n, s] - t * cap
+                place = (
+                    pl.ds(pl.multiple_of(row * BW, BW), BW),
+                    pl.ds(pl.multiple_of(col * BW, BW), BW),
+                )
+                tile = got_ref[source, q, a * BW : (a + 1) * BW, b * BW : (b + 1) * BW]
+                places.append(place)
+                sums.append(total[place] + tile.astype(jnp.float32))
+            for place, value in zip(places, sums):
+                total[place] = value
+
+        store(a).start()
+    for load in loads[2:]:
+        load.wait()
     for j in range(held):
         mine = (z * n + t) * held + j
         picked = jnp.concatenate(
@@ -447,37 +487,45 @@
             preferred_element_type=jnp.float32,
         )
         back_ref[j : j + 1, :] = scaling_ref[j : j + 1, :] * (residual_ref[j : j + 1, :] - applied)
-    for a in range(2):
-        for b in range(2):
-            store(a, b).wait()
-
-
-def assemble(n, lists, got, first_diag, steps, linking, scaling, residual):
+    store(0).wait()
+    store(1).wait()
+
+
+def assemble(n, lists, diag, linking, scaling, residual, got, steps):
     held = linking.shape[0]
-    cap = first_diag.shape[0] // BW
+    cap = diag.shape[0]
     vmem = pl.BlockSpec(memory_space=pltpu.VMEM)
+    hbm = pl.BlockSpec(memory_space=pltpu.HBM)
     return pl.pallas_call(
         functools.partial(assemble_kernel, n, held, cap),
         out_shape=(
             jax.ShapeDtypeStruct((cap * BW, cap * BW), jnp.float32),
             jax.ShapeDtypeStruct(scaling.shape, jnp.float32),
         ),
-        in_specs=[pl.BlockSpec(memory_space=pltpu.SMEM)] + [vmem] * 6,
-        out_specs=(pl.BlockSpec(memory_space=pl.ANY), vmem),
+        in_specs=[hbm] * 5 + [vmem] * 2,
+        out_specs=(hbm, vmem),
         scratch_shapes=[
             pltpu.VMEM((cap * BW, cap * BW), jnp.float32),
+            pltpu.SMEM(lists.shape, jnp.int32),
+            pltpu.VMEM(diag.shape, jnp.float32),
+            pltpu.VMEM(linking.shape, jnp.bfloat16),
+            pltpu.VMEM(scaling.shape, jnp.float32),
+            pltpu.VMEM(residual.shape, jnp.float32),
             pltpu.VMEM(steps.shape, jnp.float32),
-            pltpu.SemaphoreType.DMA((2, 2)),
+            pltpu.SemaphoreType.DMA((5,)),
+            pltpu.SemaphoreType.DMA((2,)),
         ],
-        compiler_params=pltpu.CompilerParams(vmem_limit_bytes=36 * 2**20),
+        compiler_params=pltpu.CompilerParams(vmem_limit_bytes=40 * 2**20),
         name="assemble",
-    )(lists, got, first_diag.reshape(cap, BW), steps, linking, scaling, residual)
+    )(lists, diag, linking, scaling, residual, got, steps)
 
 
 def on_square(linking, scaling, residual, blocks, step_dx, first_diag):
     n = lax.axis_size("tile")
-    got, steps = exchange(n, linking, scaling, step_dx)
-    return assemble(n, blocks.T, got, first_diag, steps, linking, scaling, residual)
+    diag = first_diag.reshape(-1, BW)
+    scaled = (jnp.sqrt(scaling)[:, :, None] * linking).astype(jnp.bfloat16)
+    got, steps = exchange(n, scaled, step_dx)
+    return assemble(n, blocks.T, diag, linking, scaling, residual, got, steps)
 
 
 def solution(mesh):

time: 84.5 us -> 80.9 us (0.957)
  local copies, waits for them, and re-layouts: 4.65 us -> 0.73 us
  other arithmetic: 0 us -> 1.46 us
  Pallas kernels: 78.9 us -> 77.8 us
    unnamed x12, local copies, waits for them, and re-layouts: 4.65 us -> 0.04 us
    pallas_call x1, Pallas kernels: 70.6 us -> 69.1 us  [exchange(): pl.pallas_call(functools.partial(exchange_kernel, n, held), out_shape=(ja...]
    convert_element_type x0 -> x1, other arithmetic: none -> 1.46 us  [on_square(): scaled = (jnp.sqrt(scaling)[:, :, None] * linking).astype(jnp.bfloat16)]
where the time goes in v3:
time: 80.9 us; the launch traced here: 80.7 us
  Pallas kernels  77.8 us (96%)
  other arithmetic  1.46 us (2%)
    pallas_call x1, Pallas kernels, exchange(): pl.pallas_call(functools.partial(exchange_kernel, n, held), out_shape=(ja...  69.1 us
    pallas_call x1, Pallas kernels, assemble(): pl.pallas_call(functools.partial(assemble_kernel, n, held, cap), out_shap...  8.7 us

profile of v3, /device:TPU:0, one launch (start us, length us, event | category | flops | bytes accessed | tf_op | source)
XLA Modules:
  0.0 80.7 jit_solution(5785857135931828260)
XLA Ops:
  0.6 0.0 copy-start.5
  0.6 0.7 sqrt.3
  1.3 1.5 %multiply_convert_fusion.scaled_ref = bf16[2,256,1024]{2,1,0:T(8,128)(2,1)S(1)} fusion(bf16[2,256,1024]{2,1,0:T(8,128)(2,1)} %linking_hbm.1, f32[2,256]{1,0:T(2,128)S(1)} %sqrt.3), kind=kLoop, calls=%fused_computation | loop fusion | flops 1572864 | bytes 2099200 | tf_op jit(solution)/shard_map/convert_element_type | solution.py:526
  2.8 0.0 copy-done.5
  2.8 0.0 copy-start
  2.8 0.0 copy-start.1
  2.8 0.0 copy-start.2
  2.8 0.0 copy-start.3
  2.9 0.0 copy-start.4
  2.9 69.1 %exchange.1 = (bf16[4,8,256,256]{3,2,1,0:T(8,128)(2,1)S(1)}, bf16[64,128]{1,0:T(8,128)(2,1)S(1)}) custom-call(bf16[2,256,1024]{2,1,0:T(8,128)(2,1)S(1)} %multiply_convert_fusion.scaled_ref, f32[16,128]{1,0:T(8,128)S(1)} %copy-done.5), custom_call_target="tpu_custom_call" | custom-call | flops 60000002048 | bytes 150000000 | tf_op jit(solution)/shard_map/exchange/pallas_call | solution.py:380
  72.0 0.0 copy-done
  72.0 0.0 copy-done.1
  72.0 0.0 copy-done.2
  72.0 0.0 copy-done.3
  72.0 0.0 copy-done.4
  72.0 8.7 %assemble.1 = (f32[2048,2048]{1,0:T(8,128)}, f32[2,256]{1,0:T(2,128)}) custom-call(s32[8,32]{1,0:T(8,128)S(1)} %bitcast.3, f32[16,128]{1,0:T(8,128)S(1)} %bitcast.2, bf16[2,256,1024]{2,1,0:T(8,128)(2,1)S(1)} %copy-done, f32[2,256]{1,0:T(2,128)S(1)} %copy-done.1, f32[2,256]{1,0:T(2,128)S(1)} %copy-done.4, ...), custom_call_target="tpu_custom_call" | custom-call | tf_op jit(solution)/shard_map/assemble/pallas_call | solution.py:499
Async XLA Ops:
  0.6 2.2 %copy-start.5 = (f32[16,128]{1,0:T(8,128)S(1)}, f32[16,128]{1,0:T(8,128)}, u32[]{:S(2)}) copy-start(f32[16,128]{1,0:T(8,128)} %step_ref.1) | copy-start | bytes 24580
  2.8 69.2 %copy-start = (bf16[2,256,1024]{2,1,0:T(8,128)(2,1)S(1)}, bf16[2,256,1024]{2,1,0:T(8,128)(2,1)}, u32[]{:S(2)}) copy-start(bf16[2,256,1024]{2,1,0:T(8,128)(2,1)} %linking_hbm.1) | copy-start | bytes 3145732
  2.8 69.2 %copy-start.1 = (f32[2,256]{1,0:T(2,128)S(1)}, f32[2,256]{1,0:T(2,128)}, u32[]{:S(2)}) copy-start(f32[2,256]{1,0:T(2,128)} %scaling_hbm.1) | copy-start | bytes 6148
  2.8 69.2 %copy-start.2 = (f32[2048]{0:T(1024)S(1)}, f32[2048]{0:T(1024)}, u32[]{:S(2)}) copy-start(f32[2048]{0:T(1024)} %param.11) | copy-start | bytes 24580
  2.8 69.2 %copy-start.3 = (s32[32,8]{0,1:T(8,128)S(1)}, s32[32,8]{0,1:T(8,128)}, u32[]{:S(2)}) copy-start(s32[32,8]{0,1:T(8,128)} %param.9) | copy-start | bytes 3076
  2.9 69.2 %copy-start.4 = (f32[2,256]{1,0:T(2,128)S(1)}, f32[2,256]{1,0:T(2,128)}, u32[]{:S(2)}) copy-start(f32[2,256]{1,0:T(2,128)} %residual_hbm.1) | copy-start | bytes 6148

commit v4 on v3

--- a/solution.py
+++ b/solution.py
@@ -108,7 +108,7 @@
 
 
 def exchange_kernel(
-    n, held, scaled_ref, step_ref, got_ref, steps_ref,
+    n, held, scaled_ref, step_ref, got_ref, steps_ref, total_ref,
     gathered, parts, end_parts, step_box,
     load_sem, own_sem, pass_sem, chain_sem, end_sem, end_got_sem, part_sem, got_sem, keep_sem,
     step_sem, step_got_sem,
@@ -298,6 +298,12 @@
     def _(j):
         to_plane(z, j)
 
+    extent = total_ref.shape[1]
+
+    @pl.loop(0, extent // 32)
+    def _(i):
+        total_ref[pl.ds(pl.multiple_of(i * 32, 32), 32), :] = jnp.zeros((32, extent), jnp.float32)
+
     @pl.when(inner)
     def _():
         @pl.loop(0, 2 * held * (n - 2))
@@ -374,7 +380,7 @@
             by_size(to == z, lambda size: part_send(q, to, size).wait_send())
 
 
-def exchange(n, scaled, step_dx):
+def exchange(n, scaled, step_dx, extent):
     held, rows, width = scaled.shape
     vmem = pl.BlockSpec(memory_space=pltpu.VMEM)
     return pl.pallas_call(
@@ -382,9 +388,10 @@
         out_shape=(
             jax.ShapeDtypeStruct((n, n * held, 2 * BW, 2 * BW), jnp.bfloat16),
             jax.ShapeDtypeStruct((n * step_dx.shape[0], BW), jnp.bfloat16),
+            jax.ShapeDtypeStruct((extent, extent), jnp.float32),
         ),
         in_specs=[pl.BlockSpec(memory_space=pl.ANY), vmem],
-        out_specs=(vmem, vmem),
+        out_specs=(vmem, vmem, vmem),
         scratch_shapes=[
             pltpu.VMEM((n, held, rows, width), jnp.bfloat16),
             pltpu.VMEM((n * held, n, 2 * BW, 2 * BW), jnp.bfloat16),
@@ -403,7 +410,7 @@
             pltpu.SemaphoreType.DMA((n,)),
         ],
         compiler_params=pltpu.CompilerParams(
-            collective_id=0, has_side_effects=True, vmem_limit_bytes=40 * 2**20
+            collective_id=0, has_side_effects=True, vmem_limit_bytes=20 * 2**20
         ),
         cost_estimate=pl.CostEstimate(
             flops=60_000_000_000, bytes_accessed=60_000_000_000 // 400, transcendentals=0
@@ -413,7 +420,7 @@
 
 
 def assemble_kernel(
-    n, held, cap, lists_hbm, diag_hbm, linking_hbm, scaling_hbm, residual_hbm, got_ref, steps_ref,
+    n, held, cap, lists_hbm, linking_hbm, scaling_hbm, residual_hbm, diag_hbm, got_ref, steps_ref, given_ref,
     schur_ref, back_ref, total, lists_ref, diag_ref, linking_ref, scaling_ref, residual_ref, wide,
     load_sem, out_sem,
 ):
@@ -421,9 +428,9 @@
     t = lax.axis_index("tile")
     span = cap // 2 * BW
 
-    def store(a):
-        rows = pl.ds(a * span, span)
-        return pltpu.make_async_copy(total.at[rows], schur_ref.at[rows], out_sem.at[a])
+    def store(a, b):
+        place = (pl.ds(a * span, span), pl.ds(b * span, span))
+        return pltpu.make_async_copy(total.at[place], schur_ref.at[place], out_sem.at[a, b])
 
     pairs = (
         (lists_hbm, lists_ref), (diag_hbm, diag_ref), (linking_hbm, linking_ref),
@@ -435,44 +442,34 @@
     for load in loads:
         load.start()
     wide[...] = steps_ref[...].astype(jnp.float32)
+    loads[0].wait()
+    loads[1].wait()
     level = pair_masks()[1]
     for a in range(2):
-
-        @pl.loop(0, span // 32)
-        def _(i):
-            rows = pl.ds(pl.multiple_of(a * span + i * 32, 32), 32)
-            total[rows, :] = jnp.zeros((32, cap * BW), jnp.float32)
-
-        if a == 0:
-            loads[0].wait()
-            loads[1].wait()
-
-        @pl.when(z == t)
-        def _():
-            for r in range(a * cap // 2, (a + 1) * cap // 2):
-                total[r * BW : (r + 1) * BW, r * BW : (r + 1) * BW] = jnp.where(
-                    level, diag_ref[r : r + 1, :], 0.0
-                )
-
-        @pl.loop(0, n * n * held, unroll=4)
-        def _(i):
-            source, q = i // (n * held), i % (n * held)
-            s = ((q // held) * n + source) * held + q % held
-            row = lists_ref[z + a * n, s] - z * cap
-            places, sums = [], []
-            for b in range(2):
+        for b in range(2):
+
+            @pl.loop(0, n * n * held, unroll=4)
+            def _(i):
+                source, q = i // (n * held), i % (n * held)
+                s = ((q // held) * n + source) * held + q % held
+                row = lists_ref[z + a * n, s] - z * cap
                 col = lists_ref[t + b * n, s] - t * cap
                 place = (
                     pl.ds(pl.multiple_of(row * BW, BW), BW),
                     pl.ds(pl.multiple_of(col * BW, BW), BW),
                 )
                 tile = got_ref[source, q, a * BW : (a + 1) * BW, b * BW : (b + 1) * BW]
-                places.append(place)
-                sums.append(total[place] + tile.astype(jnp.float32))
-            for place, value in zip(places, sums):
-                total[place] = value
-
-        store(a).start()
+                total[place] += tile.astype(jnp.float32)
+
+            if a == b:
+
+                @pl.when(z == t)
+                def _():
+                    for r in range(a * cap // 2, (a + 1) * cap // 2):
+                        place = (slice(r * BW, (r + 1) * BW), slice(r * BW, (r + 1) * BW))
+                        total[place] += jnp.where(level, diag_ref[r : r + 1, :], 0.0)
+
+            store(a, b).start()
     for load in loads[2:]:
         load.wait()
     for j in range(held):
@@ -487,25 +484,27 @@
             preferred_element_type=jnp.float32,
         )
         back_ref[j : j + 1, :] = scaling_ref[j : j + 1, :] * (residual_ref[j : j + 1, :] - applied)
-    store(0).wait()
-    store(1).wait()
-
-
-def assemble(n, lists, diag, linking, scaling, residual, got, steps):
+    for a in range(2):
+        for b in range(2):
+            store(a, b).wait()
+
+
+def assemble(n, lists, linking, scaling, residual, diag, got, steps, given):
     held = linking.shape[0]
-    cap = diag.shape[0]
+    cap = given.shape[0] // BW
     vmem = pl.BlockSpec(memory_space=pltpu.VMEM)
     hbm = pl.BlockSpec(memory_space=pltpu.HBM)
     return pl.pallas_call(
         functools.partial(assemble_kernel, n, held, cap),
         out_shape=(
-            jax.ShapeDtypeStruct((cap * BW, cap * BW), jnp.float32),
+            jax.ShapeDtypeStruct(given.shape, jnp.float32),
             jax.ShapeDtypeStruct(scaling.shape, jnp.float32),
+            jax.ShapeDtypeStruct(given.shape, jnp.float32),
         ),
-        in_specs=[hbm] * 5 + [vmem] * 2,
-        out_specs=(hbm, vmem),
+        in_specs=[hbm] * 5 + [vmem] * 3,
+        out_specs=(hbm, vmem, vmem),
+        input_output_aliases={7: 2},
         scratch_shapes=[
-            pltpu.VMEM((cap * BW, cap * BW), jnp.float32),
             pltpu.SMEM(lists.shape, jnp.int32),
             pltpu.VMEM(diag.shape, jnp.float32),
             pltpu.VMEM(linking.shape, jnp.bfloat16),
@@ -513,19 +512,19 @@
             pltpu.VMEM(residual.shape, jnp.float32),
             pltpu.VMEM(steps.shape, jnp.float32),
             pltpu.SemaphoreType.DMA((5,)),
-            pltpu.SemaphoreType.DMA((2,)),
+            pltpu.SemaphoreType.DMA((2, 2)),
         ],
-        compiler_params=pltpu.CompilerParams(vmem_limit_bytes=40 * 2**20),
+        compiler_params=pltpu.CompilerParams(vmem_limit_bytes=20 * 2**20),
         name="assemble",
-    )(lists, diag, linking, scaling, residual, got, steps)
+    )(lists, linking, scaling, residual, diag, got, steps, given)[:2]
 
 
 def on_square(linking, scaling, residual, blocks, step_dx, first_diag):
     n = lax.axis_size("tile")
     diag = first_diag.reshape(-1, BW)
     scaled = (jnp.sqrt(scaling)[:, :, None] * linking).astype(jnp.bfloat16)
-    got, steps = exchange(n, scaled, step_dx)
-    return assemble(n, blocks.T, diag, linking, scaling, residual, got, steps)
+    got, steps, given = exchange(n, scaled, step_dx, first_diag.shape[0])
+    return assemble(n, blocks.T, linking, scaling, residual, diag, got, steps, given)
 
 
 def solution(mesh):

time: 80.9 us -> 80.8 us (level)
  no operation moved by 1% of the time
where the time goes in v4:
time: 80.8 us; the launch traced here: 80.6 us
  Pallas kernels  77 us (95%)
  other arithmetic  1.46 us (2%)
  local copies, waits for them, and re-layouts  1.4 us (2%)
    pallas_call x1, Pallas kernels, exchange(): pl.pallas_call(functools.partial(exchange_kernel, n, held), out_shape=(ja...  69.1 us
    pallas_call x1, Pallas kernels, assemble(): pl.pallas_call(functools.partial(assemble_kernel, n, held, cap), out_shap...  7.95 us

profile of v4, /device:TPU:0, one launch (start us, length us, event | category | flops | bytes accessed | tf_op | source)
XLA Modules:
  0.0 80.6 jit_solution(17367285240986581266)
XLA Ops:
  0.6 0.7 sqrt.3
  1.3 1.5 %multiply_convert_fusion.scaled_ref = bf16[2,256,1024]{2,1,0:T(8,128)(2,1)S(1)} fusion(bf16[2,256,1024]{2,1,0:T(8,128)(2,1)} %linking_hbm.1, f32[2,256]{1,0:T(2,128)S(1)} %sqrt.3), kind=kLoop, calls=%fused_computation | loop fusion | flops 1572864 | bytes 2099200 | tf_op jit(solution)/shard_map/convert_element_type | solution.py:525
  2.8 0.0 copy-start.5
  2.8 0.7 copy-done.5
  3.5 0.0 copy-start
  3.5 0.0 copy-start.1
  3.5 0.0 copy-start.2
  3.5 0.0 copy-start.3
  3.5 0.0 copy-start.4
  3.5 69.1 %exchange.1 = (bf16[4,8,256,256]{3,2,1,0:T(8,128)(2,1)S(1)}, bf16[64,128]{1,0:T(8,128)(2,1)S(1)}, f32[2048,2048]{1,0:T(8,128)S(1)}) custom-call(bf16[2,256,1024]{2,1,0:T(8,128)(2,1)S(1)} %multiply_convert_fusion.scaled_ref, f32[16,128]{1,0:T(8,128)S(1)} %copy-done.5), custom_call_target="tpu_custom_call" | custom-call | flops 60000002048 | bytes 150000000 | tf_op jit(solution)/shard_map/exchange/pallas_call | solution.py:386
  72.6 0.0 copy-done
  72.6 0.0 copy-done.1
  72.6 0.0 copy-done.2
  72.6 0.0 copy-done.3
  72.7 0.0 copy-done.4
  72.7 8.0 %assemble.1 = (f32[2048,2048]{1,0:T(8,128)}, f32[2,256]{1,0:T(2,128)}, f32[2048,2048]{1,0:T(8,128)S(1)}) custom-call(s32[8,32]{1,0:T(8,128)S(1)} %bitcast.3, bf16[2,256,1024]{2,1,0:T(8,128)(2,1)S(1)} %copy-done, f32[2,256]{1,0:T(2,128)S(1)} %copy-done.2, f32[2,256]{1,0:T(2,128)S(1)} %copy-done.4, ...), custom_call_target="tpu_custom_call", output_to_operand_aliasing={{2}: (7, {})} | custom-call | tf_op jit(solution)/shard_map/assemble/pallas_call | solution.py:497
Async XLA Ops:
  2.8 0.7 copy-start.5
  3.5 69.1 %copy-start = (bf16[2,256,1024]{2,1,0:T(8,128)(2,1)S(1)}, bf16[2,256,1024]{2,1,0:T(8,128)(2,1)}, u32[]{:S(2)}) copy-start(bf16[2,256,1024]{2,1,0:T(8,128)(2,1)} %linking_hbm.1) | copy-start | bytes 3145732
  3.5 69.1 %copy-start.1 = (f32[2048]{0:T(1024)S(1)}, f32[2048]{0:T(1024)}, u32[]{:S(2)}) copy-start(f32[2048]{0:T(1024)} %param.11) | copy-start | bytes 24580
  3.5 69.1 %copy-start.2 = (f32[2,256]{1,0:T(2,128)S(1)}, f32[2,256]{1,0:T(2,128)}, u32[]{:S(2)}) copy-start(f32[2,256]{1,0:T(2,128)} %scaling_hbm.1) | copy-start | bytes 6148
  3.5 69.1 %copy-start.3 = (s32[32,8]{0,1:T(8,128)S(1)}, s32[32,8]{0,1:T(8,128)}, u32[]{:S(2)}) copy-start(s32[32,8]{0,1:T(8,128)} %param.9) | copy-start | bytes 3076
  3.5 69.2 %copy-start.4 = (f32[2,256]{1,0:T(2,128)S(1)}, f32[2,256]{1,0:T(2,128)}, u32[]{:S(2)}) copy-start(f32[2,256]{1,0:T(2,128)} %residual_hbm.1) | copy-start | bytes 6148

commit v5 on v4

--- a/solution.py
+++ b/solution.py
@@ -448,7 +448,7 @@
     for a in range(2):
         for b in range(2):
 
-            @pl.loop(0, n * n * held, unroll=4)
+            @pl.loop(0, n * n * held, unroll=8)
             def _(i):
                 source, q = i // (n * held), i % (n * held)
                 s = ((q // held) * n + source) * held + q % held

time: 80.8 us -> 80.8 us (level)
  no operation moved by 1% of the time
where the time goes in v5:
time: 80.8 us; the launch traced here: 80.6 us
  Pallas kernels  77 us (95%)
  other arithmetic  1.46 us (2%)
  local copies, waits for them, and re-layouts  1.4 us (2%)
    pallas_call x1, Pallas kernels, exchange(): pl.pallas_call(functools.partial(exchange_kernel, n, held), out_shape=(ja...  69.1 us
    pallas_call x1, Pallas kernels, assemble(): pl.pallas_call(functools.partial(assemble_kernel, n, held, cap), out_shap...  7.9 us

profile of v5, /device:TPU:0, one launch (start us, length us, event | category | flops | bytes accessed | tf_op | source)
XLA Modules:
  0.0 80.6 jit_solution(12021687704047747471)
XLA Ops:
  0.6 0.7 sqrt.3
  1.3 1.5 %multiply_convert_fusion.scaled_ref = bf16[2,256,1024]{2,1,0:T(8,128)(2,1)S(1)} fusion(bf16[2,256,1024]{2,1,0:T(8,128)(2,1)} %linking_hbm.1, f32[2,256]{1,0:T(2,128)S(1)} %sqrt.3), kind=kLoop, calls=%fused_computation | loop fusion | flops 1572864 | bytes 2099200 | tf_op jit(solution)/shard_map/convert_element_type | solution.py:525
  2.8 0.0 copy-start.5
  2.8 0.7 copy-done.5
  3.5 0.0 copy-start
  3.5 0.0 copy-start.1
  3.5 0.0 copy-start.2
  3.5 0.0 copy-start.3
  3.5 0.0 copy-start.4
  3.5 69.1 %exchange.1 = (bf16[4,8,256,256]{3,2,1,0:T(8,128)(2,1)S(1)}, bf16[64,128]{1,0:T(8,128)(2,1)S(1)}, f32[2048,2048]{1,0:T(8,128)S(1)}) custom-call(bf16[2,256,1024]{2,1,0:T(8,128)(2,1)S(1)} %multiply_convert_fusion.scaled_ref, f32[16,128]{1,0:T(8,128)S(1)} %copy-done.5), custom_call_target="tpu_custom_call" | custom-call | flops 60000002048 | bytes 150000000 | tf_op jit(solution)/shard_map/exchange/pallas_call | solution.py:386
  72.6 0.0 copy-done
  72.6 0.0 copy-done.1
  72.6 0.0 copy-done.2
  72.6 0.0 copy-done.3
  72.7 0.0 copy-done.4
  72.7 7.9 %assemble.1 = (f32[2048,2048]{1,0:T(8,128)}, f32[2,256]{1,0:T(2,128)}, f32[2048,2048]{1,0:T(8,128)S(1)}) custom-call(s32[8,32]{1,0:T(8,128)S(1)} %bitcast.3, bf16[2,256,1024]{2,1,0:T(8,128)(2,1)S(1)} %copy-done, f32[2,256]{1,0:T(2,128)S(1)} %copy-done.2, f32[2,256]{1,0:T(2,128)S(1)} %copy-done.4, ...), custom_call_target="tpu_custom_call", output_to_operand_aliasing={{2}: (7, {})} | custom-call | tf_op jit(solution)/shard_map/assemble/pallas_call | solution.py:497
Async XLA Ops:
  2.8 0.7 copy-start.5
  3.5 69.1 %copy-start = (bf16[2,256,1024]{2,1,0:T(8,128)(2,1)S(1)}, bf16[2,256,1024]{2,1,0:T(8,128)(2,1)}, u32[]{:S(2)}) copy-start(bf16[2,256,1024]{2,1,0:T(8,128)(2,1)} %linking_hbm.1) | copy-start | bytes 3145732
  3.5 69.1 %copy-start.1 = (f32[2048]{0:T(1024)S(1)}, f32[2048]{0:T(1024)}, u32[]{:S(2)}) copy-start(f32[2048]{0:T(1024)} %param.11) | copy-start | bytes 24580
  3.5 69.1 %copy-start.2 = (f32[2,256]{1,0:T(2,128)S(1)}, f32[2,256]{1,0:T(2,128)}, u32[]{:S(2)}) copy-start(f32[2,256]{1,0:T(2,128)} %scaling_hbm.1) | copy-start | bytes 6148
  3.5 69.1 %copy-start.3 = (s32[32,8]{0,1:T(8,128)S(1)}, s32[32,8]{0,1:T(8,128)}, u32[]{:S(2)}) copy-start(s32[32,8]{0,1:T(8,128)} %param.9) | copy-start | bytes 3076
  3.5 69.2 %copy-start.4 = (f32[2,256]{1,0:T(2,128)S(1)}, f32[2,256]{1,0:T(2,128)}, u32[]{:S(2)}) copy-start(f32[2,256]{1,0:T(2,128)} %residual_hbm.1) | copy-start | bytes 6148
